TPU v7x, 128 devices: a whole 4x4x4 slice. The times are simulated.
128 devices in a mesh: seq: 4 (over z), head: 32 (over y, x, core).
Axes of the slice: x: 4, y: 4, z: 4, core: 2. Of those that a mesh axis runs over, the one named last changes fastest.
Arguments:
- queries: float32 [8192, 4096], P('seq', 'head'), may hold values from -6 to 6
- key_rows: float32 [8192, 4096], P('seq', 'head'), may hold values from -6 to 6
- values: float32 [8192, 4096], P('seq', 'head'), may hold values from -6 to 6
- out_weight: bfloat16 [4096, 2048], P('head'), may hold values from -0.09375 to 0.09375
- expert_ids: int32 [8192, 8], P(('seq', 'head')), may hold values from 0 to 127, all different within a row; in each aligned block of 64 rows (0 to 63, 64 to 127, ...) at most 8 rows name the same one
- gate_ints: int32 [8192, 8], P(('seq', 'head')), may hold values from 1 to 1023
- w_gate: bfloat16 [128, 2048, 768], P(('seq', 'head')), may hold values from -0.125 to 0.125
- w_up: bfloat16 [128, 2048, 768], P(('seq', 'head')), may hold values from -0.125 to 0.125
- w_down: bfloat16 [128, 768, 2048], P(('seq', 'head')), may hold values from -0.21875 to 0.21875
Outputs:
- layer_out: float32 [8192, 2048], P(('seq', 'head'))
Inputs may be any that keep to these rules, and one draw needn't show every extreme that they name: `expert_ids`: each row names 8 different experts. Within the rows of one device (aligned blocks of 64 rows) no expert is named more than 8 times, a bound that some block reaches.
All inputs are finite; a program needn't handle non-finite values.
Results may differ from a plain program's by a relative error of at most 0.017.
Values may be sent and summed in bfloat16 or wider, within the bound.
A program may use at most 128 MiB of HBM per device.

v0:
```python
import math
import jax
import jax.numpy as jnp
from jax import lax
from jax.sharding import PartitionSpec as P

DH = 128
HIGH = lax.Precision.HIGHEST


def cut_along(array, dim, devices):
    dims = array.shape
    blocks = array.reshape(*dims[:dim], devices, dims[dim] // devices, *dims[dim + 1 :])
    return jnp.moveaxis(blocks, dim, 0)


def laid_out(blocks, dim):
    blocks = jnp.moveaxis(blocks, 0, dim)
    dims = blocks.shape
    return blocks.reshape(*dims[:dim], dims[dim] * dims[dim + 1], *dims[dim + 2 :])


def exchange_both(array, axis, axes, splits, concats):
    sizes = [lax.axis_size(a) for a in axes]
    blocks = cut_along(array, splits[0], sizes[0])
    blocks = jnp.moveaxis(cut_along(blocks, splits[1] + 1, sizes[1]), 0, 1)
    inside = blocks.shape[2:]
    blocks = blocks.reshape(-1, *inside)
    blocks = lax.all_to_all(blocks, axis, split_axis=0, concat_axis=0, tiled=True)
    blocks = laid_out(blocks.reshape(*sizes, *inside), concats[0] + 1)
    return laid_out(blocks, concats[1])


def causal_linear(query_heads, key_heads, value_heads):
    heads, length, width = query_heads.shape
    block = math.gcd(512, length)
    count = length // block

    def split(array):
        return array.reshape(heads, count, block, width).transpose(1, 0, 2, 3)

    lower = jnp.tril(jnp.ones((block, block), jnp.float32))

    def advance(state, inputs):
        query_block, key_block, value_block = inputs
        scores = jnp.einsum("hid,hjd->hij", query_block, key_block, precision=HIGH) * lower
        output = jnp.einsum("hij,hjd->hid", scores, value_block, precision=HIGH)
        output = output + jnp.einsum("hid,hde->hie", query_block, state, precision=HIGH)
        state = state + jnp.einsum("hjd,hje->hde", key_block, value_block, precision=HIGH)
        return (state, output)

    start = jnp.zeros((heads, width, width), jnp.float32)
    state, outputs = lax.scan(
        advance, start, (split(query_heads), split(key_heads), split(value_heads))
    )
    return (outputs.transpose(1, 0, 2, 3).reshape(heads, length, width), state)


def shards(queries, key_rows, values, out_weight, expert_ids, gate_ints, w_gate, w_up, w_down):
    length = queries.shape[0]
    heads_here = queries.shape[1] // DH

    def split_heads(array):
        return array.reshape(length, heads_here, DH).transpose(1, 0, 2)

    query_heads = split_heads(queries)
    local_out, local_state = causal_linear(query_heads, split_heads(key_rows), split_heads(values))
    every_state = lax.all_gather(
        local_state[None].astype(jnp.bfloat16), "seq", axis=0, tiled=True
    ).astype(jnp.float32)
    before = (jnp.arange(every_state.shape[0], dtype=jnp.int32) < lax.axis_index("seq")).astype(
        jnp.float32
    )
    earlier = jnp.sum(every_state * before[:, None, None, None], axis=0)
    heads_out = local_out + jnp.einsum("hid,hde->hie", query_heads, earlier, precision=HIGH)
    heads_out = heads_out * lax.rsqrt(
        jnp.mean(heads_out * heads_out, axis=-1, keepdims=True) + 1e-06
    )
    attn = heads_out.transpose(1, 0, 2).reshape(length, heads_here * DH).astype(jnp.bfloat16)
    head_count = lax.axis_size("head")
    seq_count = lax.axis_size("seq")
    tok_count = length // head_count
    all_heads = lax.all_to_all(attn, "head", split_axis=0, concat_axis=1, tiled=True)
    all_rows = lax.all_gather(out_weight, "head", axis=0, tiled=True)
    projected = jnp.dot(all_heads, all_rows, preferred_element_type=jnp.float32)
    normed = (
        projected * lax.rsqrt(jnp.mean(projected * projected, axis=-1, keepdims=True) + 1e-06)
    ).astype(jnp.bfloat16)
    gates = gate_ints.astype(jnp.float32)
    gates = gates / jnp.sum(gates, axis=-1, keepdims=True)
    top_count = expert_ids.shape[1]
    local_experts = w_gate.shape[0]
    devices = seq_count * head_count
    experts = local_experts * devices
    capacity = max(2, 2 * tok_count * top_count // experts)
    width = normed.shape[1]
    flat_ids = expert_ids.reshape(-1)
    assigned = flat_ids.shape[0]
    onehot = (flat_ids[:, None] == jnp.arange(experts, dtype=jnp.int32)[None, :]).astype(jnp.int32)
    before_count = jnp.cumsum(onehot, axis=0, dtype=jnp.int32) - onehot
    position = jnp.sum(before_count * onehot, axis=1, dtype=jnp.int32)
    slot_index = flat_ids * capacity + position
    source = (
        jnp.zeros((experts * capacity,), jnp.int32)
        .at[slot_index]
        .set(jnp.arange(assigned, dtype=jnp.int32))
    )
    filled = jnp.zeros((experts * capacity,), jnp.bool_).at[slot_index].set(True)
    picked = normed[source // top_count]
    outgoing = jnp.where(filled[:, None], picked, jnp.zeros_like(picked))
    outgoing = outgoing.reshape(seq_count, head_count, local_experts, capacity, width)
    received = exchange_both(outgoing, ("seq", "head"), ("seq", "head"), (0, 1), (0, 1))
    expert_received = received.reshape(devices, local_experts, capacity, width)
    gate_val = jnp.einsum(
        "nesd,edf->nesf", expert_received, w_gate, preferred_element_type=jnp.float32
    )
    up_val = jnp.einsum("nesd,edf->nesf", expert_received, w_up, preferred_element_type=jnp.float32)
    act = (jax.nn.silu(gate_val) * up_val).astype(jnp.bfloat16)
    result = jnp.einsum("nesf,efd->nesd", act, w_down, preferred_element_type=jnp.float32).astype(
        jnp.bfloat16
    )
    result = result.reshape(seq_count, head_count, local_experts, capacity, width)
    returned = exchange_both(result, ("seq", "head"), ("seq", "head"), (0, 1), (0, 1))
    returned = returned.reshape(experts * capacity, width)
    gathered = returned[slot_index].astype(jnp.float32) * gates.reshape(-1)[:, None]
    mixture = jnp.sum(gathered.reshape(tok_count, top_count, width), axis=1)
    return projected + mixture


def solution(mesh):
    placed = (
        P("seq", "head"),
        P("seq", "head"),
        P("seq", "head"),
        P("head", None),
        P(("seq", "head"), None),
        P(("seq", "head"), None),
        P(("seq", "head"), None, None),
        P(("seq", "head"), None, None),
        P(("seq", "head"), None, None),
    )
    return jax.shard_map(
        shards, mesh=mesh, in_specs=placed, out_specs=P(("seq", "head"), None), check_vma=False
    )
```

profile of v0, /device:TPU:1, one launch (start us, length us, event | category | flops | bytes accessed | tf_op | source)
XLA Modules:
  0.0 276.8 jit_solution(5523111241887061232)
XLA Ops:
  6.5 0.7 all-gather.3.cloned.1.call-update
  7.3 30.9 %while.13 = (s32[]{:T(128)}, f32[1,128,128]{2,1,0:T(8,128)S(1)}, f32[4,1,512,128]{3,2,1,0:T(8,128)}, f32[4,1,512,128]{3,2,1,0:T(8,128)}, f32[4,1,512,128]{3,2,1,...) while((s32[]{:T(128)}, f32[1,128,128]{2,1,0:T(8,128)S(1)}, ...), condition=%wide.region_1.2_spmd.clone, body=%wide.region_0.1_spmd.clone.sunk | while | flops 1007534080 | bytes 4656736 | solution.py:53
  7.3 2.2 convolution_multiply_fusion.2
  9.5 1.9 fusion.89
  11.5 2.0 fusion.90
  13.5 1.6 fusion.88
  15.1 2.0 convolution_multiply_fusion.2
  17.1 1.9 fusion.89
  19.1 2.0 fusion.90
  21.1 1.6 fusion.88
  22.8 2.1 convolution_multiply_fusion.2
  24.8 1.9 fusion.89
  26.8 2.0 fusion.90
  28.8 1.6 fusion.88
  30.5 2.0 convolution_multiply_fusion.2
  32.5 1.9 fusion.89
  34.5 2.0 fusion.90
  36.5 1.6 fusion.88
  38.2 2.6 copy.37
  40.8 12.0 %all-gather = bf16[4,128,128]{2,1,0:T(8,128)(2,1)S(1)} all-gather(bf16[1,128,128]{2,1,0:T(8,128)(2,1)S(1)} %convert_element_type.66), channel_id=2, replica_groups=mesh['seq'=4,'head'=32] {'seq'}, dimensions={0}, use_global_device_ids=true | all-gather | bytes 163840 | tf_op jit(solution)/shard_map/all_gather | solution.py:68
  52.7 0.1 fusion.50
  52.8 2.7 multiply_reduce_fusion
  55.6 0.9 multiply_convert_fusion
  56.5 2.1 copy.26
  58.6 9.8 %all-to-all-start = ((bf16[32,64,128]{2,1,0:T(8,128)(2,1)}), bf16[32,64,128]{2,1,0:T(8,128)(2,1)}, u32[]{:S(2)}, u32[]{:S(2)}) async-start(bf16[32,64,128]{2,1,0:T(8,128)(2,1)} %bitcast.182), calls=%async_computation | async-start | bytes 1048576 | tf_op jit(solution)/shard_map/all_to_all | solution.py:83
  68.6 0.1 copy.31
  68.7 0.2 fusion.51
  69.0 0.2 fusion.49
  69.5 2.4 scatter_custom_fusion.1
  71.9 2.6 scatter_custom_fusion
  74.7 9.7 %all-to-all-done = bf16[32,64,128]{2,1,0:T(8,128)(2,1)} async-done(((bf16[32,64,128]{2,1,0:T(8,128)(2,1)}), bf16[32,64,128]{2,1,0:T(8,128)(2,1)}, u32[]{:S(2)}, u32[]{:S(2)}) %all-to-all-start) | async-done | bytes 524320 | tf_op jit(solution)/shard_map/all_to_all | solution.py:83
  84.4 6.9 %all-gather.3.cloned.1.call-done = bf16[4096,2048]{1,0:T(8,128)(2,1)} async-done(((bf16[128,2048]{1,0:T(8,128)(2,1)}), bf16[4096,2048]{1,0:T(8,128)(2,1)}) %all-gather.3.cloned.1.call-update) | async-done | bytes 16777232 | tf_op jit(solution)/shard_map/all_gather | solution.py:84
  91.3 9.1 %multiply_reduce_fusion.1 = (f32[64]{0:T(128)S(1)}, f32[64,2048]{1,0:T(8,128)S(1)}) fusion(bf16[4096,2048]{1,0:T(8,128)(2,1)} %all-gather.3.cloned.1.call-done, bf16[32,64,128]{2,1,0:T(8,128)(2,1)} %all-to-all-done), kind=kOutput, calls=%fused_computation.59 | convolution fusion | flops 1074003968 | bytes 17826048 | tf_op jit(solution)/shard_map/dot_general | solution.py:85
  100.4 0.8 copy-done.1
  101.1 0.1 multiply_convert_fusion.1
  101.2 6.0 %gather_fusion = bf16[1024,2048]{1,0:T(8,128)(2,1)} fusion(bf16[64,2048]{1,0:T(8,128)(2,1)S(1)} %multiply_convert_fusion.1, s32[1024]{0:T(1024)S(1)} %fusion.55), kind=kCustom, calls=%fused_computation | custom fusion | bytes 8392704 | tf_op jit(solution)/shard_map/gather | solution.py:109
  107.3 2.5 bitcast_select_fusion
  109.8 60.2 %all_to_all.26 = bf16[128,1,1,1,8,2048]{5,4,3,2,1,0:T(8,128)(2,1)S(1)} all-to-all(bf16[128,1,1,1,8,2048]{5,4,3,2,1,0:T(8,128)(2,1)S(1)} %bitcast_select_fusion), channel_id=1, replica_groups=mesh['seq'=4,'head'=32] {'seq','head'}, dimensions={0} | all-to-all | bytes 8388608 | tf_op jit(solution)/shard_map/all_to_all | solution.py:29
  170.0 2.3 copy.34
  172.3 2.0 copy-done.2
  174.3 5.2 %fusion.30 = f32[128,8,768]{2,0,1:T(8,128)} fusion(bf16[128,8,2048]{2,0,1:T(8,128)(2,1)S(1)} %bitcast.180, bf16[1,2048,768]{2,1,0:T(8,128)(2,1)S(1)} %copy-done.5), kind=kOutput, calls=%fused_computation.41 | convolution fusion | flops 3221225472 | bytes 10485760 | tf_op jit(solution)/shard_map/nesd,edf->nesf/dot_general | solution.py:117
  179.5 12.3 %convert_bitcast_fusion = bf16[128,1,1,1,8,2048]{5,0,4,3,2,1:T(8,128)(2,1)} fusion(bf16[1,768,2048]{2,1,0:T(8,128)(2,1)S(1)} %copy-done, f32[128,8,768]{2,0,1:T(8,128)} %fusion.30, bf16[128,8,2048]{2,0,1:T(8,128)(2,1)} %bitcast.181, bf16[1,2048,768]{2,1,0:T(8,128)(2,1)} %param.17), kind=kOutput, calls=%fused_computation.37 | convolution fusion | flops 6449266688 | bytes 17825792 | tf_op jit(solution)/shard_map/nesf,efd->nesd/dot_general | solution.py:119
  191.8 6.5 %copy.35 = bf16[128,1,1,1,8,2048]{5,4,3,2,1,0:T(8,128)(2,1)} copy(bf16[128,1,1,1,8,2048]{5,0,4,3,2,1:T(8,128)(2,1)} %convert_bitcast_fusion) | data formatting | bytes 8388608 | tf_op jit(solution)/shard_map/reshape;transpose;transpose;reshape;reshape;reshape | solution.py:28
  198.3 5.6 %all-to-all-start.2 = ((bf16[128,1,1,1,8,2048]{5,4,3,2,1,0:T(8,128)(2,1)}), bf16[128,1,1,1,8,2048]{5,4,3,2,1,0:T(8,128)(2,1)}, u32[]{:S(2)}, u32[]{:S(2)}) async-start(bf16[128,1,1,1,8,2048]{5,4,3,2,1,0:T(8,128)(2,1)} %copy.35), calls=%async_computation.2 | async-start | bytes 8388608 | tf_op jit(solution)/shard_map/all_to_all | solution.py:29
  204.0 52.6 %all-to-all-done.2 = bf16[128,1,1,1,8,2048]{5,4,3,2,1,0:T(8,128)(2,1)} async-done(((bf16[128,1,1,1,8,2048]{5,4,3,2,1,0:T(8,128)(2,1)}), bf16[128,1,1,1,8,2048]{5,4,3,2,1,0:T(8,128)(2,1)}, u32[]{:S(2)}, u32[]{:S(2)}) %all-to-all-start.2) | async-done | bytes 4194336 | tf_op jit(solution)/shard_map/all_to_all | solution.py:29
  256.6 8.0 %gather_fusion.1 = bf16[512,2048]{1,0:T(8,128)(2,1)} fusion(bf16[1024,2048]{1,0:T(8,128)(2,1)} %bitcast.46, s32[1024]{0:T(1024)S(1)} %pad_clamp_fusion), kind=kCustom, calls=%fused_computation.1 | custom fusion | bytes 4196352 | tf_op jit(solution)/shard_map/gather | solution.py:125
  264.6 3.4 %fusion.27 = f32[64,2048]{1,0:T(8,128)S(1)} fusion(bf16[512,2048]{1,0:T(8,128)(2,1)} %gather_fusion.1, f32[64,8]{1,0:T(8,128)S(1)} %copy.36), kind=kLoop, calls=%fused_computation.35 | loop fusion | flops 3014656 | bytes 2623488 | tf_op jit(solution)/shard_map/reduce_sum | solution.py:126
  268.1 1.9 add.82
  (38 shorter events, 0.8 us)
Async XLA Ops:
  6.5 172.9 %copy-start = (bf16[1,768,2048]{2,1,0:T(8,128)(2,1)S(1)}, bf16[1,768,2048]{2,1,0:T(8,128)(2,1)}, u32[]{:S(2)}) copy-start(bf16[1,768,2048]{2,1,0:T(8,128)(2,1)} %param.19) | copy-start | bytes 9437188
  6.5 84.7 %all-gather.3.cloned.1.call-start = ((), (), s32[]{:S(2)}) async-start(), calls=%async_computation.3 | async-start | bytes 17301504 | tf_op jit(solution)/shard_map/all_gather | solution.py:84
  52.8 15.5 %copy-start.3 = (s32[64,8]{0,1:T(8,128)S(1)}, s32[64,8]{0,1:T(8,128)}, u32[]{:S(2)}) copy-start(s32[64,8]{0,1:T(8,128)} %param.15) | copy-start | bytes 6148
  58.6 25.8 %all-to-all-start = ((bf16[32,64,128]{2,1,0:T(8,128)(2,1)}), bf16[32,64,128]{2,1,0:T(8,128)(2,1)}, u32[]{:S(2)}, u32[]{:S(2)}) async-start(bf16[32,64,128]{2,1,0:T(8,128)(2,1)} %bitcast.182), calls=%async_computation | async-start | bytes 1048576 | tf_op jit(solution)/shard_map/all_to_all | solution.py:83
  100.3 0.8 copy-start.1
  170.0 4.3 %copy-start.5 = (bf16[1,2048,768]{2,1,0:T(8,128)(2,1)S(1)}, bf16[1,2048,768]{2,1,0:T(8,128)(2,1)}, u32[]{:S(2)}) copy-start(bf16[1,2048,768]{2,1,0:T(8,128)(2,1)} %param.18) | copy-start | bytes 9437188
  172.3 2.0 copy-start.2
  198.2 5.6 %copy-start.4 = (s32[64,8]{0,1:T(8,128)S(1)}, s32[64,8]{0,1:T(8,128)}, u32[]{:S(2)}) copy-start(s32[64,8]{0,1:T(8,128)} %param.16) | copy-start | bytes 6148
  198.3 58.4 %all-to-all-start.2 = ((bf16[128,1,1,1,8,2048]{5,4,3,2,1,0:T(8,128)(2,1)}), bf16[128,1,1,1,8,2048]{5,4,3,2,1,0:T(8,128)(2,1)}, u32[]{:S(2)}, u32[]{:S(2)}) async-start(bf16[128,1,1,1,8,2048]{5,4,3,2,1,0:T(8,128)(2,1)} %copy.35), calls=%async_computation.2 | async-start | bytes 8388608 | tf_op jit(solution)/shard_map/all_to_all | solution.py:29
Sparse Core Ops, SparseCore 0:
  9.6 81.5 all-gather.2
where the time goes:
time: 278 us; the launch traced here: 277 us
  blocking collectives  72.2 us (26%)
  waiting for transfers between devices  69.9 us (25%)
  matrix products  60 us (22%)
  local copies, waits for them, and re-layouts  36.1 us (13%)
  starting transfers between devices  15.4 us (6%)
  between operations  13.6 us (5%)
  other arithmetic  9.54 us (3%)
    all_to_all x1, blocking collectives, exchange_both(): lax.all_to_all(blocks, axis, split_axis=0, concat_axis=0, tiled=True)  60.2 us
    all_to_all x1, waiting for transfers between devices, exchange_both(): lax.all_to_all(blocks, axis, split_axis=0, concat_axis=0, tiled=True)  52.6 us
    dot_general x1, matrix products, shards(): jnp.einsum('nesf,efd->nesd', act, w_down, preferred_element_type=jnp.floa...  12.3 us
    all_gather x1, blocking collectives, shards(): lax.all_gather(local_state[None].astype(jnp.bfloat16), 'seq', axis=0, til...  12 us
    all_to_all x1, starting transfers between devices, shards(): lax.all_to_all(attn, 'head', split_axis=0, concat_axis=1, tiled=True)  9.76 us
    all_to_all x1, waiting for transfers between devices, shards(): lax.all_to_all(attn, 'head', split_axis=0, concat_axis=1, tiled=True)  9.66 us
    dot_general x1, matrix products, shards(): projected = jnp.dot(all_heads, all_rows, preferred_element_type=jnp.float32)  9.08 us
    dot_general x4, matrix products, advance(): jnp.einsum('hid,hjd->hij', query_block, key_block, precision=HIGH) * lower  8.3 us
  transfers between devices with their start and end apart: 3, of which 3 were waited for; matrix products, arithmetic and copies ran while one was open for 16% of the time, Pallas kernels for 0%

commit v1 on v0

--- a/solution.py
+++ b/solution.py
@@ -81,7 +81,9 @@
     seq_count = lax.axis_size("seq")
     tok_count = length // head_count
     all_heads = lax.all_to_all(attn, "head", split_axis=0, concat_axis=1, tiled=True)
-    all_rows = lax.all_gather(out_weight, "head", axis=0, tiled=True)
+    all_rows = jnp.concatenate(
+        lax.all_to_all(jnp.stack([out_weight] * lax.axis_size("head")), "head", 0, 0), axis=0
+    )
     projected = jnp.dot(all_heads, all_rows, preferred_element_type=jnp.float32)
     normed = (
         projected * lax.rsqrt(jnp.mean(projected * projected, axis=-1, keepdims=True) + 1e-06)

time: 278 us -> 474 us (1.71)
  waiting for transfers between devices: 69.9 us -> 248 us
  blocking collectives: 72.2 us -> 103 us
  between operations: 13.6 us -> 0.21 us
  local copies, waits for them, and re-layouts: 36.1 us -> 42.6 us
    all_to_all x1, waiting for transfers between devices: 9.66 us -> 195 us  [shards(): lax.all_to_all(jnp.stack([out_weight] * lax.axis_size('head')), 'head', 0...]
    all_to_all x0 -> x1, blocking collectives: none -> 21.8 us  [shards(): lax.all_to_all(attn, 'head', split_axis=0, concat_axis=1, tiled=True)]
    all_to_all x1, blocking collectives: 60.2 us -> 69.1 us  [exchange_both(): lax.all_to_all(blocks, axis, split_axis=0, concat_axis=0, tiled=True)]
    all_gather x1 -> x0, waiting for transfers between devices: 6.9 us -> none  [shards(): all_rows = lax.all_gather(out_weight, 'head', axis=0, tiled=True)]
    another operation x3 -> x4, local copies, waits for them, and re-layouts: 0.03 us -> 6.81 us  [the longest x1 6.78 us: shards(): jnp.stack([out_weight] * lax.axis_size('head'))]
  transfers between devices with their start and end apart: 3 -> 2, of which waited for: 3 -> 2; matrix products, arithmetic and copies ran while one was open for 16% -> 1% of each run, Pallas kernels for 0% -> 0%
where the time goes in v1:
time: 474 us; the launch traced here: 472 us
  waiting for transfers between devices  248 us (52%)
  blocking collectives  103 us (22%)
  matrix products  58.4 us (12%)
  local copies, waits for them, and re-layouts  42.6 us (9%)
  starting transfers between devices  10.9 us (2%)
  other arithmetic  9.54 us (2%)
    all_to_all x1, waiting for transfers between devices, shards(): lax.all_to_all(jnp.stack([out_weight] * lax.axis_size('head')), 'head', 0...  195 us
    all_to_all x1, blocking collectives, exchange_both(): lax.all_to_all(blocks, axis, split_axis=0, concat_axis=0, tiled=True)  69.1 us
    all_to_all x1, waiting for transfers between devices, exchange_both(): lax.all_to_all(blocks, axis, split_axis=0, concat_axis=0, tiled=True)  52.6 us
    all_to_all x1, blocking collectives, shards(): lax.all_to_all(attn, 'head', split_axis=0, concat_axis=1, tiled=True)  21.8 us
    dot_general x1, matrix products, shards(): jnp.einsum('nesf,efd->nesd', act, w_down, preferred_element_type=jnp.floa...  12.3 us
    all_gather x1, blocking collectives, shards(): lax.all_gather(local_state[None].astype(jnp.bfloat16), 'seq', axis=0, til...  11.6 us
  transfers between devices with their start and end apart: 2, of which 2 were waited for; matrix products, arithmetic and copies ran while one was open for 1% of the time, Pallas kernels for 0%

profile of v1, /device:TPU:1, one launch (start us, length us, event | category | flops | bytes accessed | tf_op | source)
XLA Modules:
  0.0 472.3 jit_solution(7150347223014566401)
XLA Ops:
  0.0 30.8 %while.13 = (s32[]{:T(128)}, f32[1,128,128]{2,1,0:T(8,128)S(1)}, f32[4,1,512,128]{3,2,1,0:T(8,128)}, f32[4,1,512,128]{3,2,1,0:T(8,128)}, f32[4,1,512,128]{3,2,1,...) while((s32[]{:T(128)}, f32[1,128,128]{2,1,0:T(8,128)S(1)}, ...), condition=%wide.region_1.2_spmd.clone, body=%wide.region_0.1_spmd.clone.sunk | while | flops 1007534080 | bytes 4657258 | solution.py:53
  0.0 2.2 convolution_multiply_fusion.2
  2.2 1.9 fusion.86
  4.1 2.0 fusion.87
  6.1 1.6 fusion.85
  7.8 2.0 convolution_multiply_fusion.2
  9.8 1.9 fusion.86
  11.8 2.0 fusion.87
  13.8 1.6 fusion.85
  15.5 2.0 convolution_multiply_fusion.2
  17.5 1.9 fusion.86
  19.4 2.0 fusion.87
  21.5 1.6 fusion.85
  23.1 2.0 convolution_multiply_fusion.2
  25.1 1.9 fusion.86
  27.1 2.0 fusion.87
  29.1 1.6 fusion.85
  30.8 2.6 copy.36
  33.4 11.6 %all-gather = bf16[4,128,128]{2,1,0:T(8,128)(2,1)S(1)} all-gather(bf16[1,128,128]{2,1,0:T(8,128)(2,1)S(1)} %convert_element_type.66), channel_id=2, replica_groups=mesh['seq'=4,'head'=32] {'seq'}, dimensions={0}, use_global_device_ids=true | all-gather | bytes 163840 | tf_op jit(solution)/shard_map/all_gather | solution.py:68
  45.0 0.1 fusion.48
  45.1 2.7 multiply_reduce_fusion
  47.7 0.9 multiply_convert_fusion
  48.6 2.0 copy.26
  50.6 21.8 %all_to_all.28 = bf16[32,64,128]{2,1,0:T(8,128)(2,1)} all-to-all(bf16[32,64,128]{2,1,0:T(8,128)(2,1)} %bitcast.179), channel_id=1, replica_groups=mesh['seq'=4,'head'=32] {'head'}, dimensions={0} | all-to-all | bytes 1048576 | tf_op jit(solution)/shard_map/all_to_all | solution.py:83
  72.5 6.8 %stack.2 = bf16[32,128,2048]{2,1,0:T(8,128)(2,1)} broadcast(bf16[128,2048]{1,0:T(8,128)(2,1)} %param.14), dimensions={1,2} | broadcast | bytes 17301504 | tf_op jit(solution)/shard_map/stack | solution.py:85
  79.3 5.3 %all-to-all-start.1 = ((bf16[32,128,2048]{2,1,0:T(8,128)(2,1)}), bf16[32,128,2048]{2,1,0:T(8,128)(2,1)}, u32[]{:S(2)}, u32[]{:S(2)}) async-start(bf16[32,128,2048]{2,1,0:T(8,128)(2,1)} %stack.2), calls=%async_computation.1 | async-start | bytes 33554432 | tf_op jit(solution)/shard_map/all_to_all | solution.py:85
  85.1 0.1 copy.30
  85.2 0.2 fusion.49
  85.5 0.2 fusion.47
  85.8 2.4 scatter_custom_fusion.1
  88.2 2.4 scatter_custom_fusion
  90.8 195.3 %all-to-all-done.1 = bf16[32,128,2048]{2,1,0:T(8,128)(2,1)} async-done(((bf16[32,128,2048]{2,1,0:T(8,128)(2,1)}), bf16[32,128,2048]{2,1,0:T(8,128)(2,1)}, u32[]{:S(2)}, u32[]{:S(2)}) %all-to-all-start.1) | async-done | bytes 16777248 | tf_op jit(solution)/shard_map/all_to_all | solution.py:85
  286.1 7.6 %multiply_reduce_fusion.1 = (f32[64]{0:T(128)S(1)}, f32[64,2048]{1,0:T(8,128)S(1)}) fusion(bf16[32,128,2048]{2,1,0:T(8,128)(2,1)} %all-to-all-done.1, bf16[32,64,128]{2,1,0:T(8,128)(2,1)} %all_to_all.28), kind=kOutput, calls=%fused_computation.58 | convolution fusion | flops 1074003968 | bytes 17826048 | tf_op jit(solution)/shard_map/dot_general | solution.py:87
  293.8 0.8 copy-done.1
  294.5 0.1 multiply_convert_fusion.1
  294.6 6.0 %gather_fusion = bf16[1024,2048]{1,0:T(8,128)(2,1)} fusion(bf16[64,2048]{1,0:T(8,128)(2,1)S(1)} %multiply_convert_fusion.1, s32[1024]{0:T(1024)S(1)} %fusion.53), kind=kCustom, calls=%fused_computation | custom fusion | bytes 8392704 | tf_op jit(solution)/shard_map/gather | solution.py:111
  300.7 2.5 bitcast_select_fusion
  303.2 69.1 %all_to_all.29 = bf16[128,1,1,1,8,2048]{5,4,3,2,1,0:T(8,128)(2,1)S(1)} all-to-all(bf16[128,1,1,1,8,2048]{5,4,3,2,1,0:T(8,128)(2,1)S(1)} %bitcast_select_fusion), channel_id=1, replica_groups=mesh['seq'=4,'head'=32] {'seq','head'}, dimensions={0} | all-to-all | bytes 8388608 | tf_op jit(solution)/shard_map/all_to_all | solution.py:29
  372.3 2.3 copy.33
  374.7 2.0 copy-done.2
  376.6 5.2 %fusion.30 = f32[128,8,768]{2,0,1:T(8,128)} fusion(bf16[128,8,2048]{2,0,1:T(8,128)(2,1)S(1)} %bitcast.177, bf16[1,2048,768]{2,1,0:T(8,128)(2,1)S(1)} %copy-done.5), kind=kOutput, calls=%fused_computation.41 | convolution fusion | flops 3221225472 | bytes 10485760 | tf_op jit(solution)/shard_map/nesd,edf->nesf/dot_general | solution.py:119
  381.8 12.3 %convert_bitcast_fusion = bf16[128,1,1,1,8,2048]{5,0,4,3,2,1:T(8,128)(2,1)} fusion(bf16[1,768,2048]{2,1,0:T(8,128)(2,1)S(1)} %copy-done, f32[128,8,768]{2,0,1:T(8,128)} %fusion.30, bf16[128,8,2048]{2,0,1:T(8,128)(2,1)} %bitcast.178, bf16[1,2048,768]{2,1,0:T(8,128)(2,1)} %param.17), kind=kOutput, calls=%fused_computation.37 | convolution fusion | flops 6449266688 | bytes 17825792 | tf_op jit(solution)/shard_map/nesf,efd->nesd/dot_general | solution.py:121
  394.1 6.5 %copy.34 = bf16[128,1,1,1,8,2048]{5,4,3,2,1,0:T(8,128)(2,1)} copy(bf16[128,1,1,1,8,2048]{5,0,4,3,2,1:T(8,128)(2,1)} %convert_bitcast_fusion) | data formatting | bytes 8388608 | tf_op jit(solution)/shard_map/reshape;transpose;transpose;reshape;reshape;reshape | solution.py:28
  400.6 5.6 %all-to-all-start.3 = ((bf16[128,1,1,1,8,2048]{5,4,3,2,1,0:T(8,128)(2,1)}), bf16[128,1,1,1,8,2048]{5,4,3,2,1,0:T(8,128)(2,1)}, u32[]{:S(2)}, u32[]{:S(2)}) async-start(bf16[128,1,1,1,8,2048]{5,4,3,2,1,0:T(8,128)(2,1)} %copy.34), calls=%async_computation.3 | async-start | bytes 8388608 | tf_op jit(solution)/shard_map/all_to_all | solution.py:29
  406.3 52.6 %all-to-all-done.3 = bf16[128,1,1,1,8,2048]{5,4,3,2,1,0:T(8,128)(2,1)} async-done(((bf16[128,1,1,1,8,2048]{5,4,3,2,1,0:T(8,128)(2,1)}), bf16[128,1,1,1,8,2048]{5,4,3,2,1,0:T(8,128)(2,1)}, u32[]{:S(2)}, u32[]{:S(2)}) %all-to-all-start.3) | async-done | bytes 4194336 | tf_op jit(solution)/shard_map/all_to_all | solution.py:29
  459.0 8.0 %gather_fusion.1 = bf16[512,2048]{1,0:T(8,128)(2,1)} fusion(bf16[1024,2048]{1,0:T(8,128)(2,1)} %bitcast.47, s32[1024]{0:T(1024)S(1)} %pad_clamp_fusion), kind=kCustom, calls=%fused_computation.1 | custom fusion | bytes 4196352 | tf_op jit(solution)/shard_map/gather | solution.py:127
  467.0 3.4 fusion.27
  470.4 1.9 add.82
  (37 shorter events, 0.8 us)
Async XLA Ops:
  0.0 381.8 %copy-start = (bf16[1,768,2048]{2,1,0:T(8,128)(2,1)S(1)}, bf16[1,768,2048]{2,1,0:T(8,128)(2,1)}, u32[]{:S(2)}) copy-start(bf16[1,768,2048]{2,1,0:T(8,128)(2,1)} %param.19) | copy-start | bytes 9437188
  79.3 5.3 %copy-start.3 = (s32[64,8]{0,1:T(8,128)S(1)}, s32[64,8]{0,1:T(8,128)}, u32[]{:S(2)}) copy-start(s32[64,8]{0,1:T(8,128)} %param.15) | copy-start | bytes 6148
  79.3 206.8 %all-to-all-start.1 = ((bf16[32,128,2048]{2,1,0:T(8,128)(2,1)}), bf16[32,128,2048]{2,1,0:T(8,128)(2,1)}, u32[]{:S(2)}, u32[]{:S(2)}) async-start(bf16[32,128,2048]{2,1,0:T(8,128)(2,1)} %stack.2), calls=%async_computation.1 | async-start | bytes 33554432 | tf_op jit(solution)/shard_map/all_to_all | solution.py:85
  293.7 0.8 copy-start.1
  372.3 4.3 copy-start.5
  374.6 2.0 copy-start.2
  400.6 5.6 %copy-start.4 = (s32[64,8]{0,1:T(8,128)S(1)}, s32[64,8]{0,1:T(8,128)}, u32[]{:S(2)}) copy-start(s32[64,8]{0,1:T(8,128)} %param.16) | copy-start | bytes 6148
  400.6 58.4 %all-to-all-start.3 = ((bf16[128,1,1,1,8,2048]{5,4,3,2,1,0:T(8,128)(2,1)}), bf16[128,1,1,1,8,2048]{5,4,3,2,1,0:T(8,128)(2,1)}, u32[]{:S(2)}, u32[]{:S(2)}) async-start(bf16[128,1,1,1,8,2048]{5,4,3,2,1,0:T(8,128)(2,1)} %copy.34), calls=%async_computation.3 | async-start | bytes 8388608 | tf_op jit(solution)/shard_map/all_to_all | solution.py:29
